TPU v7x, 32 devices: a whole 2x2x4 slice. The times are simulated.
32 devices in a mesh: groups: 2 (over x), din: 8 (over z, y), dout: 2 (over core).
Axes of the slice: x: 2, y: 2, z: 4, core: 2. Of those that a mesh axis runs over, the one named last changes fastest.
Arguments:
- tokens: bfloat16 [2048, 16384], P(('groups', 'din'), 'dout'), parts along dimension 0, may hold values from -6 to 6
- w_query: bfloat16 [16384, 8192], P('dout', 'din'), may hold values from -0.046875 to 0.046875
- w_key: bfloat16 [16384, 512], P('dout', 'din'), may hold values from -0.046875 to 0.046875
- w_value: bfloat16 [16384, 512], P('dout', 'din'), may hold values from -0.046875 to 0.046875
- w_out: bfloat16 [8192, 16384], P('din', 'dout'), may hold values from -1 to 1
- k_cache: bfloat16 [8, 2048, 128], P('groups', 'din'), parts along dimension 0, may hold values from -1000 to 1000
- v_cache: bfloat16 [8, 2048, 128], P('groups', 'din'), parts along dimension 0, may hold values from -6 to 6
- span_start: int32 [2], P('groups'), parts along dimension 0, may hold values from 1 to 2048
Outputs:
- attended: bfloat16 [2048, 16384], P(('groups', 'din'), 'dout'), parts along dimension 0
There are 2 independent parts, one for each index of `groups`. A program takes and returns all parts, laid end to end along the dimension named above; an argument that names none is the same for every part. Nothing has to cross between parts.
All inputs are finite; a program needn't handle non-finite values.
Results may differ from a plain program's by a relative error of at most 0.014.
The roundings to bfloat16 on the way count: a program that leaves them out, or rounds other values in their place, can miss the bound.
Values may be sent and summed in bfloat16 or wider, within the bound.
A program may use at most 192 MiB of HBM per device.

v0:
```python
import math

import jax
import jax.numpy as jnp
from jax import lax
from jax.sharding import PartitionSpec as P

rope_base = 500000.0


def rotate(values, positions):
    half = values.shape[-1] // 2
    freq = jnp.exp(
        jnp.arange(half, dtype=jnp.float32) * (-2.0 * math.log(rope_base) / values.shape[-1])
    )
    angle = positions.astype(jnp.float32)[:, None] * freq[None, :]
    cosine = jnp.cos(angle)
    sine = jnp.sin(angle)
    first = values[..., :half]
    second = values[..., half:]
    return jnp.concatenate([first * cosine - second * sine, second * cosine + first * sine], -1)


def local(tokens, w_query, w_key, w_value, w_out, k_cache, v_cache, span_start):
    head_size = k_cache.shape[2]
    kv_heads = k_cache.shape[0]
    dout_count = lax.axis_size("dout")
    din_index = lax.axis_index("din")
    dout_index = lax.axis_index("dout")
    local_cols = w_query.shape[1]
    local_heads = local_cols // head_size
    key_cols = w_key.shape[1]
    scale = head_size ** (-0.5)
    piece = lax.all_gather(tokens, "din", axis=0, tiled=True)
    partial_value = jnp.concatenate(
        [
            jnp.dot(piece, w_query, preferred_element_type=jnp.float32),
            jnp.dot(piece, w_key, preferred_element_type=jnp.float32),
            jnp.dot(piece, w_value, preferred_element_type=jnp.float32),
        ],
        1,
    )
    span = partial_value.shape[0]
    query_part = lax.psum_scatter(
        partial_value[:, :local_cols], "dout", scatter_dimension=0, tiled=True
    )
    kv_part = lax.psum(partial_value[:, local_cols:].astype(jnp.bfloat16), "dout").astype(
        jnp.float32
    )
    key_full, value_full = (
        lax.all_gather(
            kv_part[:, :key_cols].astype(jnp.bfloat16), "din", axis=1, tiled=True
        ).astype(jnp.float32),
        lax.all_gather(
            kv_part[:, key_cols:].astype(jnp.bfloat16), "din", axis=1, tiled=True
        ).astype(jnp.float32),
    )
    start_pos = span_start[0]
    positions = start_pos + jnp.arange(span, dtype=jnp.int32)
    new_keys = rotate(
        key_full.reshape(span, kv_heads, head_size).transpose(1, 0, 2), positions
    ).astype(jnp.bfloat16)
    new_values = (
        value_full.reshape(span, kv_heads, head_size).transpose(1, 0, 2).astype(jnp.bfloat16)
    )
    query_rows = span // dout_count
    query_first = dout_index * query_rows
    query_pos = start_pos + query_first + jnp.arange(query_rows, dtype=jnp.int32)
    queries = rotate(
        query_part.reshape(query_rows, local_heads, head_size).transpose(1, 0, 2), query_pos
    ).astype(jnp.bfloat16)
    kv_ids = (din_index * local_heads + jnp.arange(local_heads, dtype=jnp.int32)) % kv_heads
    my_keys = jnp.take(new_keys, kv_ids, 0)
    my_values = jnp.take(new_values, kv_ids, 0)
    scores = (
        jnp.einsum("hqd,hkd->hqk", queries, my_keys, preferred_element_type=jnp.float32) * scale
    )
    causal = (
        jnp.arange(span, dtype=jnp.int32)[None, :]
        <= (query_first + jnp.arange(query_rows, dtype=jnp.int32))[:, None]
    )
    scores = jnp.where(causal[None], scores, -jnp.inf)
    peak = jnp.max(scores, -1)
    weights = jnp.exp(scores - peak[..., None])
    total = jnp.sum(weights, -1)
    weighted = jnp.einsum(
        "hqk,hkd->hqd", weights.astype(jnp.bfloat16), my_values, preferred_element_type=jnp.float32
    )
    piece_keys = jnp.take(lax.all_gather(k_cache, "din", axis=1, tiled=True), kv_ids, 0)
    piece_values = jnp.take(lax.all_gather(v_cache, "din", axis=1, tiled=True), kv_ids, 0)
    piece_scores = (
        jnp.einsum("hqd,hkd->hqk", queries, piece_keys, preferred_element_type=jnp.float32) * scale
    )
    valid = jnp.arange(piece_keys.shape[1], dtype=jnp.int32) < start_pos
    piece_scores = jnp.where(valid[None, None, :], piece_scores, -jnp.inf)
    new_peak = jnp.maximum(peak, jnp.max(piece_scores, -1))
    piece_weights = jnp.exp(piece_scores - new_peak[..., None])
    factor = jnp.exp(peak - new_peak)
    new_total = total * factor + jnp.sum(piece_weights, -1)
    new_weighted = weighted * factor[..., None] + jnp.einsum(
        "hqk,hkd->hqd",
        piece_weights.astype(jnp.bfloat16),
        piece_values,
        preferred_element_type=jnp.float32,
    )
    heads_out = (new_weighted / new_total[..., None]).astype(jnp.bfloat16)
    local_out = heads_out.transpose(1, 0, 2).reshape(query_rows, local_cols)
    head_rows = lax.all_gather(local_out, "dout", axis=0, tiled=True)
    return lax.psum_scatter(
        jnp.dot(head_rows, w_out, preferred_element_type=jnp.float32).astype(jnp.bfloat16),
        "din",
        scatter_dimension=0,
        tiled=True,
    )


def solution(mesh):
    return jax.shard_map(
        local,
        mesh=mesh,
        in_specs=(
            P(("groups", "din"), "dout"),
            P("dout", "din"),
            P("dout", "din"),
            P("dout", "din"),
            P("din", "dout"),
            P("groups", "din", None),
            P("groups", "din", None),
            P("groups"),
        ),
        out_specs=P(("groups", "din"), "dout"),
        check_vma=False,
    )
```

profile of v0, /device:TPU:0, one launch (start us, length us, event | category | flops | bytes accessed | tf_op | source)
XLA Modules:
  0.0 882.8 jit_solution(2966891323883221792)
XLA Ops:
  6.5 0.7 all-gather.7.cloned.1.call-update
  7.3 0.0 all-reduce.2.cloned.1.call-start
  7.3 232.5 %all-gather.7.cloned.1.call-done = bf16[1024,8192]{1,0:T(8,128)(2,1)} async-done(((bf16[128,8192]{1,0:T(8,128)(2,1)}), bf16[1024,8192]{1,0:T(8,128)(2,1)}) %all-gather.7.cloned.1.call-update) | async-done | bytes 16777232 | tf_op jit(solution)/shard_map/all_gather | solution.py:34
  239.8 11.1 %convolution_convert_fusion.1 = bf16[1024,64]{0,1:T(8,128)(2,1)S(1)} fusion(bf16[1024,8192]{1,0:T(8,128)(2,1)} %all-gather.7.cloned.1.call-done, bf16[8192,64]{0,1:T(8,128)(2,1)S(1)} %copy-done), kind=kOutput, calls=%fused_computation.41 | convolution fusion | flops 1073807360 | bytes 17956864 | tf_op jit(solution)/shard_map/dot_general | solution.py:39
  251.0 5.2 convolution_convert_fusion.2
  256.2 0.7 pad_maximum_fusion.2
  256.9 0.0 all-gather.13.cloned.1.call-start
  257.0 0.7 all-gather.13.cloned.1.call-update
  257.6 0.0 all-gather.15.cloned.1.call-start
  257.7 0.5 all-gather.15.cloned.1.call-update
  258.2 0.0 all-gather.9.cloned.1.call-start
  258.3 15.2 %all-reduce.2.cloned.1.call-done = bf16[1024,128]{0,1:T(8,128)(2,1)} async-done(((bf16[1024,128]{0,1:T(8,128)(2,1)}), bf16[1024,128]{0,1:T(8,128)(2,1)}) %all-reduce.2.cloned.1.call-update) | async-done | bytes 262160 | tf_op jit(solution)/shard_map/psum | solution.py:47
  273.5 1.7 fusion.45
  275.2 0.0 all-gather.9.cloned.1.call-update
  275.2 0.0 all-gather.11.cloned.1.call-start
  275.3 0.5 all-gather.11.cloned.1.call-update
  275.8 0.0 reduce-scatter.3.cloned.1.call-start
  275.8 23.5 %fusion.46 = f32[1024,1024]{1,0:T(8,128)} fusion(bf16[1024,8192]{1,0:T(8,128)(2,1)} %all-gather.7.cloned.1.call-done, bf16[8192,1024]{1,0:T(8,128)(2,1)} %param.13), kind=kOutput, calls=%fused_computation.79 | convolution fusion | flops 17179869184 | bytes 37748736 | tf_op jit(solution)/shard_map/dot_general | solution.py:37
  299.4 0.2 all-gather.17.cloned.1.call-start
  300.4 1.2 iota_compare_fusion
  301.5 1.7 multiply_cosine_fusion.1
  303.3 1.9 multiply_cosine_fusion
  305.1 21.3 %all-gather.13.cloned.1.call-done = bf16[4,2048,128]{2,1,0:T(8,128)(2,1)} async-done(((bf16[4,256,128]{2,1,0:T(8,128)(2,1)}), bf16[4,2048,128]{2,1,0:T(8,128)(2,1)}) %all-gather.13.cloned.1.call-update) | async-done | bytes 2097168 | tf_op jit(solution)/shard_map/all_gather | solution.py:89
  326.4 4.6 gather_fusion.2
  331.0 45.5 %all-gather.15.cloned.1.call-done = bf16[4,2048,128]{2,1,0:T(8,128)(2,1)} async-done(((bf16[4,256,128]{2,1,0:T(8,128)(2,1)}), bf16[4,2048,128]{2,1,0:T(8,128)(2,1)}) %all-gather.15.cloned.1.call-update) | async-done | bytes 2097168 | tf_op jit(solution)/shard_map/all_gather | solution.py:90
  376.5 4.7 gather_fusion.3
  381.2 36.1 %all-gather.9.cloned.1.call-done = bf16[1024,512]{0,1:T(8,128)(2,1)} async-done(((bf16[1024,64]{0,1:T(8,128)(2,1)}), bf16[1024,512]{0,1:T(8,128)(2,1)}) %all-gather.9.cloned.1.call-update) | async-done | bytes 1048592 | tf_op jit(solution)/shard_map/all_gather | solution.py:51
  417.3 1.5 copy.12
  418.8 0.7 subtract_convert_fusion
  419.6 0.6 pad_maximum_fusion.1
  420.1 2.1 gather_fusion
  422.3 36.2 %all-gather.11.cloned.1.call-done = bf16[1024,512]{0,1:T(8,128)(2,1)} async-done(((bf16[1024,64]{0,1:T(8,128)(2,1)}), bf16[1024,512]{0,1:T(8,128)(2,1)}) %all-gather.11.cloned.1.call-update) | async-done | bytes 1048592 | tf_op jit(solution)/shard_map/all_gather | solution.py:54
  458.5 3.3 gather_fusion.1
  461.7 9.9 %reduce-scatter.3.cloned.1.call-done = f32[512,1024]{1,0:T(8,128)} async-done(((f32[1024,1024]{1,0:T(8,128)}), f32[512,1024]{1,0:T(8,128)}) %reduce-scatter.3.cloned.1.call-update) | async-done | bytes 2097168 | tf_op jit(solution)/shard_map/reduce_scatter | solution.py:44
  471.7 1.7 bitcast_bitcast_fusion
  473.4 1.7 subtract_convert_fusion.1
  475.1 0.8 copy-done.4
  476.0 15.2 %fusion = (f32[8,512]{1,0:T(8,128)S(1)}, f32[8,512,2048]{2,1,0:T(8,128)}) fusion(pred[2048]{0:T(1024)(128)(4,1)S(1)} %iota_compare_fusion.1, bf16[8,2048,128]{2,1,0:T(8,128)(2,1)S(1)} %copy-done.4, pred[8]{0:T(512)(128)(4,1)S(1)} %compare_and_fusion, bf16[8,512,64]{2,1,0:T(8,128)(2,1)} %get-tuple-element.12, bf16[8,512,64]{2,1,0:T(8,128)(2,1)S(1)} %get-tuple-element.11), kind=kOutput, calls=%fused_computation.6 | convolution fusion | flops 2176839680 | bytes 38815752 | tf_op jit(solution)/shard_map/hqd,hkd->hqk/dot_general | solution.py:92
  491.2 11.3 %fusion.6 = (f32[8,512]{1,0:T(8,128)S(1)}, f32[8,512,1024]{2,1,0:T(8,128)}) fusion(pred[512,1024]{1,0:T(8,128)(4,1)S(1)} %copy-done.5, bf16[8,1024,128]{2,1,0:T(8,128)(2,1)} %gather_fusion, pred[8]{0:T(512)(128)(4,1)S(1)} %compare_and_fusion, bf16[8,512,64]{2,1,0:T(8,128)(2,1)} %get-tuple-element.12, bf16[8,512,64]{2,1,0:T(8,128)(2,1)S(1)} %get-tuple-element.11), kind=kOutput, calls=%fused_computation.14 | convolution fusion | flops 1089466368 | bytes 20463624 | tf_op jit(solution)/shard_map/hqd,hkd->hqk/dot_general | solution.py:76
  502.5 14.5 %fusion.1 = f32[8,512]{1,0:T(8,128)S(1)} fusion(f32[8,512,2048]{2,1,0:T(8,128)} %get-tuple-element.22, f32[8,512]{1,0:T(8,128)S(1)} %max.18, pred[2048]{0:T(1024)(128)(4,1)S(1)} %iota_compare_fusion.1), kind=kLoop, calls=%fused_computation.7 | loop fusion | flops 33550336 | bytes 33589248 | tf_op jit(solution)/shard_map/reduce_sum | solution.py:99
  516.9 17.0 %fusion.3 = f32[8,512,128]{1,2,0:T(8,128)} fusion(f32[8,512,2048]{2,1,0:T(8,128)} %get-tuple-element.22, f32[8,512]{1,0:T(8,128)S(1)} %max.18, pred[2048]{0:T(1024)(128)(4,1)S(1)} %iota_compare_fusion.1, bf16[8,2048,128]{2,1,0:T(8,128)(2,1)} %gather_fusion.3, pred[8]{0:T(512)(128)(4,1)S(1)} %compare_and_fusion), kind=kOutput, calls=%fused_computation.11 | convolution fusion | flops 2183135232 | bytes 39864328 | tf_op jit(solution)/shard_map/hqk,hkd->hqd/dot_general | solution.py:100
  533.9 8.3 fusion.7
  542.2 2.3 copy-done.3
  544.5 7.7 fusion.18
  552.3 0.0 reduce-scatter.5.cloned.1.call-start
  552.3 12.0 %all-gather.17.cloned.1.call-done = bf16[1024,1024]{0,1:T(8,128)(2,1)} async-done(((bf16[512,1024]{0,1:T(8,128)(2,1)}), bf16[1024,1024]{0,1:T(8,128)(2,1)}) %all-gather.17.cloned.1.call-update) | async-done | bytes 2097168 | tf_op jit(solution)/shard_map/all_gather | solution.py:108
  564.3 27.5 %convolution_convert_fusion = bf16[1024,8192]{1,0:T(8,128)(2,1)} fusion(bf16[1024,1024]{0,1:T(8,128)(2,1)} %all-gather.17.cloned.1.call-done, bf16[1024,8192]{1,0:T(8,128)(2,1)} %param.16), kind=kOutput, calls=%fused_computation.13 | convolution fusion | flops 17188257792 | bytes 35651584 | tf_op jit(solution)/shard_map/dot_general | solution.py:110
  591.9 284.0 %reduce-scatter.5.cloned.1.call-done = bf16[128,8192]{1,0:T(8,128)(2,1)} async-done(((bf16[1024,8192]{1,0:T(8,128)(2,1)}), bf16[128,8192]{1,0:T(8,128)(2,1)}) %reduce-scatter.5.cloned.1.call-update) | async-done | bytes 2097168 | tf_op jit(solution)/shard_map/reduce_scatter | solution.py:109
  (29 shorter events, 0.2 us)
Async XLA Ops:
  6.5 233.3 %copy-start = (bf16[8192,64]{0,1:T(8,128)(2,1)S(1)}, bf16[8192,64]{0,1:T(8,128)(2,1)}, u32[]{:S(2)}) copy-start(bf16[8192,64]{0,1:T(8,128)(2,1)} %param.15) | copy-start | bytes 3145732
  6.5 233.3 %all-gather.7.cloned.1.call-start = ((), (), s32[]{:S(2)}) async-start(), calls=%async_computation.2 | async-start | bytes 18874368 | tf_op jit(solution)/shard_map/all_gather | solution.py:34
  7.3 243.7 %copy-start.6 = (bf16[8192,64]{0,1:T(8,128)(2,1)S(1)}, bf16[8192,64]{0,1:T(8,128)(2,1)}, u32[]{:S(2)}) copy-start(bf16[8192,64]{0,1:T(8,128)(2,1)} %param.14) | copy-start | bytes 3145732
  7.3 266.2 %all-reduce.2.cloned.1.call-start = ((), (), s32[]{:S(2)}) async-start(), calls=%async_computation.4 | async-start | bytes 524288 | tf_op jit(solution)/shard_map/psum | solution.py:47
  239.8 11.1 %copy-start.2 = (bf16[1024,8192]{1,0:T(8,128)(2,1)S(1)}, bf16[1024,8192]{1,0:T(8,128)(2,1)}, u32[]{:S(2)}) copy-start(bf16[1024,8192]{1,0:T(8,128)(2,1)} %all-gather.7.cloned.1.call-done) | copy-start | bytes 50331652
  256.9 69.5 %all-gather.13.cloned.1.call-start = ((), (), s32[]{:S(2)}) async-start(), calls=%async_computation.7 | async-start | bytes 2359296 | tf_op jit(solution)/shard_map/all_gather | solution.py:89
  257.6 118.8 %all-gather.15.cloned.1.call-start = ((), (), s32[]{:S(2)}) async-start(), calls=%async_computation.8 | async-start | bytes 2359296 | tf_op jit(solution)/shard_map/all_gather | solution.py:90
  258.2 159.1 %all-gather.9.cloned.1.call-start = ((), (), s32[]{:S(2)}) async-start(), calls=%async_computation.5 | async-start | bytes 1179648 | tf_op jit(solution)/shard_map/all_gather | solution.py:51
  275.2 183.3 %all-gather.11.cloned.1.call-start = ((), (), s32[]{:S(2)}) async-start(), calls=%async_computation.6 | async-start | bytes 1179648 | tf_op jit(solution)/shard_map/all_gather | solution.py:54
  275.8 195.9 %reduce-scatter.3.cloned.1.call-start = ((), (), s32[]{:S(2)}) async-start(), calls=%async_computation.3 | async-start | bytes 6291456 | tf_op jit(solution)/shard_map/reduce_scatter | solution.py:44
  299.4 265.0 %all-gather.17.cloned.1.call-start = ((), (), s32[]{:S(2)}) async-start(), calls=%async_computation.9 | async-start | bytes 3145728 | tf_op jit(solution)/shard_map/all_gather | solution.py:108
  458.5 14.9 %copy-start.7 = (f32[512,64]{1,0:T(8,128)S(1)}, f32[512,64]{1,0:T(8,128)}, u32[]{:S(2)}) copy-start(f32[512,64]{1,0:T(8,128)} %get-tuple-element.18) | copy-start | bytes 393220
  473.4 2.6 copy-start.4
  476.0 15.2 %copy-start.5 = (pred[512,1024]{1,0:T(8,128)(4,1)S(1)}, pred[512,1024]{1,0:T(8,128)(4,1)}, u32[]{:S(2)}) copy-start(pred[512,1024]{1,0:T(8,128)(4,1)} %iota_compare_fusion) | copy-start | bytes 1572868
  533.9 10.6 %copy-start.3 = (f32[8,512,1024]{2,1,0:T(8,128)S(1)}, f32[8,512,1024]{2,1,0:T(8,128)}, u32[]{:S(2)}) copy-start(f32[8,512,1024]{2,1,0:T(8,128)} %get-tuple-element.20) | copy-start | bytes 50331652
  552.3 323.6 %reduce-scatter.5.cloned.1.call-start = ((), (), s32[]{:S(2)}) async-start(), calls=%async_computation.10 | async-start | bytes 18874368 | tf_op jit(solution)/shard_map/reduce_scatter | solution.py:109
  591.9 284.0 %copy-start.1 = (bf16[8192,64]{0,1:T(8,128)(2,1)S(1)}, bf16[8192,64]{0,1:T(8,128)(2,1)}, u32[]{:S(2)}) copy-start(bf16[8192,64]{0,1:T(8,128)(2,1)} %param.15) | copy-start | bytes 3145732
Sparse Core Ops, SparseCore 0:
  9.5 230.2 all-gather.6
  257.0 16.4 all-reduce.1
  275.9 50.4 all-gather.12
  328.7 47.7 all-gather.14
  378.7 38.6 all-gather.8
  419.5 38.8 all-gather.10
  460.9 10.7 reduce-scatter.2
  552.4 11.8 all-gather.16
  592.0 283.8 reduce-scatter.4
where the time goes:
time: 891 us; the launch traced here: 883 us
  waiting for transfers between devices  695 us (78%)
  matrix products  119 us (13%)
  other arithmetic  31.3 us (4%)
  local copies, waits for them, and re-layouts  22.8 us (3%)
  between operations  14.5 us (2%)
    reduce_scatter x1, waiting for transfers between devices, local(): lax.psum_scatter(jnp.dot(head_rows, w_out, preferred_element_type=jnp.flo...  284 us
    all_gather x1, waiting for transfers between devices, local(): piece = lax.all_gather(tokens, 'din', axis=0, tiled=True)  233 us
    all_gather x1, waiting for transfers between devices, local(): lax.all_gather(v_cache, 'din', axis=1, tiled=True)  45.5 us
    all_gather x1, waiting for transfers between devices, local(): lax.all_gather(kv_part[:, key_cols:].astype(jnp.bfloat16), 'din', axis=1,...  36.2 us
    all_gather x1, waiting for transfers between devices, local(): lax.all_gather(kv_part[:, :key_cols].astype(jnp.bfloat16), 'din', axis=1,...  36.1 us
    dot_general x1, matrix products, local(): jnp.dot(head_rows, w_out, preferred_element_type=jnp.float32)  27.5 us
    dot_general x1, matrix products, local(): jnp.dot(piece, w_query, preferred_element_type=jnp.float32)  23.5 us
    all_gather x1, waiting for transfers between devices, local(): lax.all_gather(k_cache, 'din', axis=1, tiled=True)  21.3 us
  transfers between devices with their start and end apart: 9, of which 9 were waited for; matrix products, arithmetic and copies ran while one was open for 5% of the time, Pallas kernels for 0%

commit v1 on v0

v1 whole, which is shorter than its diff:
```python
import functools
import math

import jax
import jax.numpy as jnp
from jax import lax
from jax.experimental import pallas as pl
from jax.experimental.pallas import tpu as pltpu
from jax.sharding import PartitionSpec as P

rope_base = 500000.0
MESH = pl.DeviceIdType.MESH
VMEM_BYTES = 60 * 2**20


def ring_index(pos, n, snake):
    if not snake:
        return pos
    high = pos // (n // 2)
    return (1 - high) * 2 * pos + high * (2 * (n - 1 - pos) + 1)


def ring_place(index, n, snake):
    if not snake:
        return index
    odd = index % 2
    return (1 - odd) * (index // 2) + odd * (n - 1 - index // 2)


def enter(right, left, core):
    barrier = pltpu.get_barrier_semaphore()
    for target in ({"din": right}, {"din": left}, {"dout": 1 - core}):
        pl.semaphore_signal(barrier, inc=1, device_id=target, device_id_type=MESH)
    pl.semaphore_wait(barrier, 3)


def rope_tables(positions, head_size):
    half = head_size // 2
    freq = jnp.exp(
        jnp.arange(half, dtype=jnp.float32) * (-2.0 * math.log(rope_base) / head_size)
    )
    angle = positions.astype(jnp.float32)[:, None] * freq[None, :]
    return jnp.cos(angle), jnp.sin(angle)


def rotate(values, cosine, sine):
    half = values.shape[-1] // 2
    first = values[..., :half]
    second = values[..., half:]
    return jnp.concatenate([first * cosine - second * sine, second * cosine + first * sine], -1)


def gather_kernel(
    n, snake, pair,
    x_ref, wq_hbm, wkv_hbm, k_ref, v_ref,
    out_ref, kc_ref, vc_ref,
    buf, wq, wkv, part, other,
    local_sem, send_sem, recv_sem, pair_send, pair_recv,
):
    core = lax.axis_index("dout")
    me_index = lax.axis_index("din")
    me = ring_place(me_index, n, snake)
    at = lambda pos: ring_index(lax.rem(pos + 2 * n, n), n, snake)
    right, left = at(me + 1), at(me - 1)
    rows = x_ref.shape[0]
    half = rows // 2
    slots = k_ref.shape[1]
    heads = kc_ref.shape[0]
    cols = wq.shape[1]
    own_cols = cols // 2
    steps = n // 2

    mine_heads = pl.ds(core * heads, heads)
    first = [
        x_ref.at[pl.ds(0, half)],
        k_ref.at[mine_heads],
        x_ref.at[pl.ds(half, half)],
        v_ref.at[mine_heads],
    ]

    def place(index, piece):
        if piece == 0:
            return buf.at[index, pl.ds(0, half)]
        if piece == 2:
            return buf.at[index, pl.ds(half, half)]
        ref = kc_ref if piece == 1 else vc_ref
        return ref.at[:, pl.ds(pl.multiple_of(index * slots, slots), slots)]

    locals_ = [
        pltpu.make_async_copy(first[piece], place(me_index, piece), local_sem.at[piece])
        for piece in range(4)
    ] + [
        pltpu.make_async_copy(wq_hbm, wq, local_sem.at[4]),
        pltpu.make_async_copy(wkv_hbm, wkv, local_sem.at[5]),
    ]

    def copy(way, step, piece):
        index = at(me - step if way == 0 else me + step)
        return pltpu.make_async_remote_copy(
            src_ref=first[piece] if step == 0 else place(index, piece),
            dst_ref=place(index, piece),
            send_sem=send_sem.at[way, step, piece],
            recv_sem=recv_sem.at[way, step, piece],
            device_id={"din": right if way == 0 else left},
            device_id_type=MESH,
        )

    def arrival(way, step, piece):
        index = at(me - 1 - step if way == 0 else me + 1 + step)
        return pltpu.make_async_remote_copy(
            src_ref=place(index, piece),
            dst_ref=place(index, piece),
            send_sem=send_sem.at[way, step, piece],
            recv_sem=recv_sem.at[way, step, piece],
            device_id={"din": right if way == 0 else left},
            device_id_type=MESH,
        )

    def travels(way, step, piece):
        return step < steps - 1 or (piece // 2 == way)

    def swap(order, index):
        at_rows = pl.ds(pl.multiple_of(index * rows, rows), rows)
        return pltpu.make_async_remote_copy(
            src_ref=part.at[at_rows],
            dst_ref=other.at[at_rows],
            send_sem=pair_send.at[order],
            recv_sem=pair_recv.at[order],
            device_id={"dout": 1 - core},
            device_id_type=MESH,
        )

    def project(order, index):
        at_rows = pl.ds(pl.multiple_of(index * rows, rows), rows)

        @pl.loop(0, own_cols // pair)
        def _(m):
            to = pl.ds(pl.multiple_of(m * pair, pair), pair)
            mine = pl.ds(pl.multiple_of((2 * m + core) * pair, pair), pair)
            theirs = pl.ds(pl.multiple_of((2 * m + 1 - core) * pair, pair), pair)
            part[at_rows, to] = jnp.dot(
                buf[index], wq[:, theirs], preferred_element_type=jnp.float32
            )
            out_ref[at_rows, to] = jnp.dot(
                buf[index], wq[:, mine], preferred_element_type=jnp.float32
            )

        both = jnp.dot(buf[index], wkv[...], preferred_element_type=jnp.float32)
        part[at_rows, own_cols:] = both
        out_ref[at_rows, own_cols:] = both
        swap(order, index).start()

    for item in locals_:
        item.start()
    enter(right, left, core)

    order = 0
    swaps = []
    for step in range(steps):
        for piece in range(4):
            for way in range(2):
                if step > 0:
                    arrival(way, step - 1, piece).wait_recv()
                if travels(way, step, piece):
                    copy(way, step, piece).start()
        if step == 0:
            for item in locals_:
                item.wait()
            todo = [me_index]
        else:
            todo = [at(me - step), at(me + step)]
        for index in todo:
            project(order, index)
            swaps.append((order, index))
            order += 1
    for piece in range(4):
        arrival(piece // 2, steps - 1, piece).wait_recv()
    index = at(me + steps)
    project(order, index)
    swaps.append((order, index))

    for step in range(steps):
        for piece in range(4):
            for way in range(2):
                if travels(way, step, piece):
                    copy(way, step, piece).wait_send()
    for order, index in swaps:
        swap(order, index).wait()

    @pl.loop(0, n)
    def _(block):
        at_rows = pl.ds(pl.multiple_of(block * rows, rows), rows)
        out_ref[at_rows, :] = out_ref[at_rows, :] + other[at_rows, :]


def gather_project(tokens, w_query, w_kv, k_cache, v_cache, n, snake):
    rows, features = tokens.shape
    cols = w_query.shape[1]
    kv_cols = w_kv.shape[1]
    kv_heads, slots, head_size = k_cache.shape
    heads = kv_heads // 2
    pair = heads * head_size
    width = cols // 2 + kv_cols
    any_ = pl.BlockSpec(memory_space=pl.ANY)
    cache = jax.ShapeDtypeStruct((heads, n * slots, head_size), k_cache.dtype)
    return pl.pallas_call(
        functools.partial(gather_kernel, n, snake, pair),
        out_shape=(jax.ShapeDtypeStruct((n * rows, width), jnp.float32), cache, cache),
        in_specs=[any_] * 5,
        out_specs=(pl.BlockSpec(memory_space=pltpu.VMEM), any_, any_),
        scratch_shapes=[
            pltpu.VMEM((n, rows, features), tokens.dtype),
            pltpu.VMEM((features, cols), w_query.dtype),
            pltpu.VMEM((features, kv_cols), w_kv.dtype),
            pltpu.VMEM((n * rows, width), jnp.float32),
            pltpu.VMEM((n * rows, width), jnp.float32),
            pltpu.SemaphoreType.DMA((6,)),
            pltpu.SemaphoreType.DMA((2, n // 2, 4)),
            pltpu.SemaphoreType.DMA((2, n // 2, 4)),
            pltpu.SemaphoreType.DMA((n,)),
            pltpu.SemaphoreType.DMA((n,)),
        ],
        compiler_params=pltpu.CompilerParams(
            collective_id=0, has_side_effects=True, vmem_limit_bytes=VMEM_BYTES
        ),
        name="gather_project",
    )(tokens, w_query, w_kv, k_cache, v_cache)


def attend_kernel(scale, start_ref, q_ref, kc_ref, vc_ref, nk_ref, nv_ref, out_ref):
    block = q_ref.shape[1]
    query = q_ref[0]
    contract = (((1,), (1,)), ((), ()))
    start = start_ref[0]
    old = lax.dot_general(query, kc_ref[0], contract, preferred_element_type=jnp.float32)
    new = lax.dot_general(query, nk_ref[0], contract, preferred_element_type=jnp.float32)
    slot = lax.broadcasted_iota(jnp.int32, old.shape, 1)
    old = jnp.where(slot < start, old, -jnp.inf)
    row = lax.broadcasted_iota(jnp.int32, new.shape, 0) + pl.program_id(1) * block
    col = lax.broadcasted_iota(jnp.int32, new.shape, 1)
    new = jnp.where(col <= row, new, -jnp.inf)
    peak = jnp.maximum(
        jnp.max(old, -1, keepdims=True), jnp.max(new, -1, keepdims=True)
    )
    old = jnp.exp((old - peak) * scale)
    new = jnp.exp((new - peak) * scale)
    total = jnp.sum(old, -1, keepdims=True) + jnp.sum(new, -1, keepdims=True)
    weighted = jnp.dot(
        old.astype(jnp.bfloat16), vc_ref[0], preferred_element_type=jnp.float32
    ) + jnp.dot(new.astype(jnp.bfloat16), nv_ref[0], preferred_element_type=jnp.float32)
    out_ref[...] = (weighted / total).astype(out_ref.dtype)


def attend(start, queries, old_keys, old_values, new_keys, new_values):
    heads, span, head_size = queries.shape
    groups, slots, _ = old_keys.shape
    block = 256
    old = pl.BlockSpec((1, slots, head_size), lambda h, q: (h % groups, 0, 0))
    new = pl.BlockSpec((1, span, head_size), lambda h, q: (h % groups, 0, 0))
    return pl.pallas_call(
        functools.partial(attend_kernel, head_size ** (-0.5)),
        grid=(heads, span // block),
        out_shape=jax.ShapeDtypeStruct((span, heads * head_size), jnp.bfloat16),
        in_specs=[
            pl.BlockSpec(memory_space=pltpu.SMEM),
            pl.BlockSpec((1, block, head_size), lambda h, q: (h, q, 0)),
            old, old, new, new,
        ],
        out_specs=pl.BlockSpec((block, head_size), lambda h, q: (q, h)),
        compiler_params=pltpu.CompilerParams(vmem_limit_bytes=VMEM_BYTES),
        name="attend",
    )(start, queries, old_keys, old_values, new_keys, new_values)


def scatter_kernel(
    n, snake, pair,
    h_ref, w_hbm, out_ref,
    merged, w, sums, own,
    local_sem, send_sem, recv_sem, pair_send, pair_recv,
):
    core = lax.axis_index("dout")
    me_index = lax.axis_index("din")
    me = ring_place(me_index, n, snake)
    at = lambda pos: ring_index(lax.rem(pos + 2 * n, n), n, snake)
    right, left = at(me + 1), at(me - 1)
    rows, width = out_ref.shape
    half = rows // 2
    steps = n // 2
    pairs = h_ref.shape[1] // pair
    tile = 512

    weights = pltpu.make_async_copy(w_hbm, w, local_sem.at[pairs])
    weights.start()
    enter(right, left, core)
    swaps, keeps = [], []
    for m in range(pairs):
        source = h_ref.at[:, pl.ds(m * pair, pair)]
        to = merged.at[:, pl.ds(pl.multiple_of((2 * m + core) * pair, pair), pair)]
        theirs = merged.at[:, pl.ds(pl.multiple_of((2 * m + 1 - core) * pair, pair), pair)]
        keeps.append(pltpu.make_async_copy(source, to, local_sem.at[m]))
        keeps[-1].start()
        pltpu.make_async_remote_copy(
            src_ref=source, dst_ref=to,
            send_sem=pair_send.at[m], recv_sem=pair_recv.at[m],
            device_id={"dout": 1 - core}, device_id_type=MESH,
        ).start()
        swaps.append(
            pltpu.make_async_remote_copy(
                src_ref=source, dst_ref=theirs,
                send_sem=pair_send.at[m], recv_sem=pair_recv.at[m],
                device_id={"dout": 1 - core}, device_id_type=MESH,
            )
        )

    part_rows = [pl.ds(0, half), pl.ds(half, half)]

    def multiply(way, index):
        source = pl.ds(pl.multiple_of(index * rows, rows), rows)

        @pl.loop(0, width // tile)
        def _(j):
            to = pl.ds(pl.multiple_of(j * tile, tile), tile)
            own[way, :, to] = jnp.dot(
                merged[source, :], w[:, to], preferred_element_type=jnp.float32
            )

    def copy(way, step, piece):
        return pltpu.make_async_remote_copy(
            src_ref=sums.at[way, step, part_rows[piece]],
            dst_ref=sums.at[way, step + 1, part_rows[piece]],
            send_sem=send_sem.at[way, step, piece],
            recv_sem=recv_sem.at[way, step, piece],
            device_id={"din": right if way == 0 else left},
            device_id_type=MESH,
        )

    def travels(way, step, piece):
        return step > 0 or piece == way

    for item in keeps:
        item.wait()
    for item in swaps:
        item.wait()
    weights.wait()

    for step in range(steps):
        if step == 0:
            multiply(0, at(me + steps))
        for piece in range(2):
            for way in range(2):
                if not travels(way, step, piece):
                    continue
                source = own.at[0 if step == 0 else way]
                if step > 0 and travels(way, step - 1, piece):
                    copy(way, step - 1, piece).wait_recv()
                    sums[way, step, part_rows[piece]] = (
                        sums[way, step, part_rows[piece]].astype(jnp.float32)
                        + source[part_rows[piece]]
                    ).astype(sums.dtype)
                else:
                    sums[way, step, part_rows[piece]] = source[part_rows[piece]].astype(sums.dtype)
                copy(way, step, piece).start()
        if step < steps - 1:
            multiply(0, at(me + steps - step - 1))
            multiply(1, at(me - (steps - step - 1)))
        else:
            multiply(0, me_index)
    for piece in range(2):
        for way in range(2):
            copy(way, steps - 1, piece).wait_recv()
        block = part_rows[piece]
        out_ref[block] = (
            own[0, block]
            + sums[0, steps, block].astype(jnp.float32)
            + sums[1, steps, block].astype(jnp.float32)
        ).astype(out_ref.dtype)
    for step in range(steps):
        for piece in range(2):
            for way in range(2):
                if travels(way, step, piece):
                    copy(way, step, piece).wait_send()


def project_scatter(heads_out, w_out, pair, n, snake):
    span, own_cols = heads_out.shape
    cols, width = w_out.shape
    rows = span // n
    any_ = pl.BlockSpec(memory_space=pl.ANY)
    pairs = own_cols // pair
    return pl.pallas_call(
        functools.partial(scatter_kernel, n, snake, pair),
        out_shape=jax.ShapeDtypeStruct((rows, width), jnp.bfloat16),
        in_specs=[any_, any_],
        out_specs=pl.BlockSpec(memory_space=pltpu.VMEM),
        scratch_shapes=[
            pltpu.VMEM((span, cols), jnp.bfloat16),
            pltpu.VMEM((cols, width), w_out.dtype),
            pltpu.VMEM((2, n // 2 + 1, rows, width), jnp.bfloat16),
            pltpu.VMEM((2, rows, width), jnp.float32),
            pltpu.SemaphoreType.DMA((pairs + 1,)),
            pltpu.SemaphoreType.DMA((2, n // 2, 2)),
            pltpu.SemaphoreType.DMA((2, n // 2, 2)),
            pltpu.SemaphoreType.DMA((pairs,)),
            pltpu.SemaphoreType.DMA((pairs,)),
        ],
        compiler_params=pltpu.CompilerParams(
            collective_id=1, has_side_effects=True, vmem_limit_bytes=VMEM_BYTES
        ),
        name="project_scatter",
    )(heads_out, w_out)


def local(n, snake, tokens, w_query, w_key, w_value, w_out, k_cache, v_cache, span_start):
    kv_heads, _, head_size = k_cache.shape
    core = lax.axis_index("dout")
    heads = kv_heads // 2
    pair = heads * head_size
    own_cols = w_query.shape[1] // 2
    key_cols = w_key.shape[1]
    span = n * tokens.shape[0]
    cosine, sine = rope_tables(span_start[0] + jnp.arange(span, dtype=jnp.int32), head_size)
    w_kv = jnp.concatenate([w_key, w_value], 1)
    sums, old_keys, old_values = gather_project(
        tokens, w_query, w_kv, k_cache, v_cache, n, snake
    )
    kv = lax.all_gather(sums[:, own_cols:].astype(jnp.bfloat16), "din", axis=0)
    queries = sums[:, :own_cols].reshape(span, own_cols // head_size, head_size)
    queries = rotate(queries.transpose(1, 0, 2), cosine, sine).astype(jnp.bfloat16)

    def mine(block):
        whole = block.reshape(2, n // 2, span, key_cols)
        part = lax.dynamic_index_in_dim(whole, core, 0, keepdims=False)
        part = part.transpose(1, 0, 2).reshape(span, heads, head_size)
        return part.transpose(1, 0, 2)

    new_keys = rotate(mine(kv[:, :, :key_cols]).astype(jnp.float32), cosine, sine).astype(
        jnp.bfloat16
    )
    new_values = mine(kv[:, :, key_cols:])
    heads_out = attend(span_start, queries, old_keys, old_values, new_keys, new_values)
    return project_scatter(heads_out, w_out, pair, n, snake)


def solution(mesh):
    n = mesh.shape["din"]
    snake = n == 8
    return jax.shard_map(
        functools.partial(local, n, snake),
        mesh=mesh,
        in_specs=(
            P(("groups", "din"), "dout"),
            P("dout", "din"),
            P("dout", "din"),
            P("dout", "din"),
            P("din", "dout"),
            P("groups", "din", None),
            P("groups", "din", None),
            P("groups"),
        ),
        out_specs=P(("groups", "din"), "dout"),
        check_vma=False,
    )
```

time: 891 us -> 480 us (0.54)
  waiting for transfers between devices: 695 us -> 39.3 us
  Pallas kernels: 0 us -> 392 us
  matrix products: 119 us -> 0 us
  other arithmetic: 31.3 us -> 10.9 us
    pallas_call x0 -> x3, Pallas kernels: none -> 392 us  [the longest x1 190 us: gather_project(): pl.pallas_call(functools.partial(gather_kernel, n, snake, pair), out_shap...]
    all_gather x6 -> x1, waiting for transfers between devices: 384 us -> 39.3 us  [local(): kv = lax.all_gather(sums[:, own_cols:].astype(jnp.bfloat16), 'din', axis=0)]
    reduce_scatter x2 -> x0, waiting for transfers between devices: 294 us -> none  [the longest x1 284 us: local(): lax.psum_scatter(jnp.dot(head_rows, w_out, preferred_element_type=jnp.flo...]
    dot_general x8 -> x0, matrix products: 119 us -> none  [the longest x1 27.5 us: local(): jnp.dot(head_rows, w_out, preferred_element_type=jnp.float32)]
    reduce_sum x2 -> x0, other arithmetic: 22.7 us -> none  [the longest x1 14.5 us: local(): new_total = total * factor + jnp.sum(piece_weights, -1)]
    psum x1 -> x0, waiting for transfers between devices: 15.2 us -> none  [local(): lax.psum(partial_value[:, local_cols:].astype(jnp.bfloat16), 'dout')]
    gather x4 -> x0, local copies, waits for them, and re-layouts: 14.7 us -> none  [the longest x1 4.74 us: local(): jnp.take(lax.all_gather(v_cache, 'din', axis=1, tiled=True), kv_ids, 0)]
    slice x1 -> x5, local copies, waits for them, and re-layouts: 1.68 us -> 11.2 us  [the longest x1 4.27 us: local(): new_values = mine(kv[:, :, key_cols:])]
  transfers between devices with their start and end apart: 9 -> 1, of which waited for: 9 -> 1; matrix products, arithmetic and copies ran while one was open for 5% -> 2% of each run, Pallas kernels for 0% -> 0%
where the time goes in v1:
time: 480 us
  Pallas kernels  392 us (82%)
  waiting for transfers between devices  39.3 us (8%)
  local copies, waits for them, and re-layouts  23 us (5%)
  between operations  14.2 us (3%)
  other arithmetic  10.9 us (2%)
    pallas_call x1, Pallas kernels, gather_project(): pl.pallas_call(functools.partial(gather_kernel, n, snake, pair), out_shap...  190 us
    pallas_call x1, Pallas kernels, project_scatter(): pl.pallas_call(functools.partial(scatter_kernel, n, snake, pair), out_sha...  172 us
    all_gather x1, waiting for transfers between devices, local(): kv = lax.all_gather(sums[:, own_cols:].astype(jnp.bfloat16), 'din', axis=0)  39.3 us
    pallas_call x1, Pallas kernels, attend(): pl.pallas_call(functools.partial(attend_kernel, head_size ** (-0.5)), gri...  30.7 us
  transfers between devices with their start and end apart: 1, of which 1 were waited for; matrix products, arithmetic and copies ran while one was open for 2% of the time, Pallas kernels for 0%

profile of v1, /device:TPU:0, one launch (start us, length us, event | category | flops | bytes accessed | tf_op | source)
XLA Modules:
  0.0 479.6 jit_solution(9767879598970751392)
XLA Ops:
  6.5 0.0 copy-start.1
  6.5 0.0 all-gather.3.cloned.1.call-start
  6.5 2.1 copy.12
  8.7 0.0 copy-done.1
  8.7 1.8 copy.11
  10.4 4.1 pad_maximum_fusion.wkv_hbm
  14.5 189.6 %gather_project.1 = (f32[1024,640]{1,0:T(8,128)}, bf16[2,2048,128]{2,1,0:T(8,128)(2,1)}, bf16[2,2048,128]{2,1,0:T(8,128)(2,1)}) custom-call(bf16[128,8192]{1,0:T(8,128)(2,1)} %x_ref.1, bf16[8192,1024]{1,0:T(8,128)(2,1)} %wq_hbm.1, bf16[8192,128]{1,0:T(8,128)(2,1)} %pad_maximum_fusion.wkv_hbm, bf16[4,256,128]{2,1,0:T(8,128)(2,1)} %k_ref.1, ...), custom_call_target="tpu_custom_call" | custom-call | tf_op jit(solution)/shard_map/gather_project/pallas_call | solution.py:206
  204.1 1.8 slice.49
  205.8 0.0 all-gather.3.cloned.1.call-update
  205.9 1.8 slice.25
  208.3 1.8 copy.13
  210.1 1.9 copy.14
  212.0 1.9 multiply_cosine_fusion
  213.9 0.7 subtract_convert_fusion
  214.7 1.5 pad_maximum_fusion.1.q_ref
  216.2 39.3 %all-gather.3.cloned.1.call-done = bf16[8192,128]{1,0:T(8,128)(2,1)} async-done(((bf16[1024,128]{1,0:T(8,128)(2,1)}), bf16[8192,128]{1,0:T(8,128)(2,1)}) %all-gather.3.cloned.1.call-update) | async-done | bytes 2097168 | tf_op jit(solution)/shard_map/all_gather | solution.py:426
  255.5 4.3 fusion
  259.8 1.6 copy.15
  261.4 1.1 bitcast_convert_fusion
  262.5 0.3 copy.16
  262.8 0.0 copy-start
  262.9 0.4 subtract_convert_fusion.1
  263.3 1.2 copy-done
  264.4 0.1 constant_dynamic-slice_fusion
  264.5 0.3 copy.19
  264.8 1.0 copy.18
  265.8 1.1 pad_maximum_fusion.2.nk_ref
  267.0 30.7 %attend.1.h_ref = bf16[1024,512]{1,0:T(8,128)(2,1)} custom-call(s32[1]{0:T(128)} %copy.21.start_ref, bf16[4,1024,128]{2,1,0:T(8,128)(2,1)} %pad_maximum_fusion.1.q_ref, bf16[2,2048,128]{2,1,0:T(8,128)(2,1)} %get-tuple-element.9.kc_ref, bf16[2,2048,128]{2,1,0:T(8,128)(2,1)} %get-tuple-element.10.vc_ref, bf16[2,1024,128]{2,1,0:T(8,128)(2,1)} %pad_maximum_fusion.2.nk_ref, ...), custom_call_target="tpu_custom_call" | custom-call | tf_op jit(solution)/shard_map/attend/pallas_call | solution.py:260
  297.7 172.0 %project_scatter.1 = bf16[128,8192]{1,0:T(8,128)(2,1)} custom-call(bf16[1024,512]{1,0:T(8,128)(2,1)} %attend.1.h_ref, bf16[1024,8192]{1,0:T(8,128)(2,1)} %w_hbm.1), custom_call_target="tpu_custom_call" | custom-call | tf_op jit(solution)/shard_map/project_scatter/pallas_call | solution.py:390
  469.7 3.1 copy.22
  (2 shorter events, 0.0 us)
Async XLA Ops:
  6.5 2.1 copy-start.1
  6.5 248.9 %all-gather.3.cloned.1.call-start = ((), (), s32[]{:S(2)}) async-start(), calls=%async_computation | async-start | bytes 2359296 | tf_op jit(solution)/shard_map/all_gather | solution.py:426
  262.8 1.6 copy-start
Sparse Core Ops, SparseCore 0:
  206.0 49.4 all-gather.2
